TPU v7x, 512 devices: a whole 4x4x16 slice. The times are simulated.
512 devices in a mesh: dp: 4 (over y), wide: 64 (over z, x), mp: 2 (over core).
Axes of the slice: x: 4, y: 4, z: 16, core: 2. Of those that a mesh axis runs over, the one named last changes fastest.
Arguments:
- neighbour_rows: bfloat16 [2048, 16, 896], P(('dp', 'wide')), parts along dimension 0, may hold values from -6 to 6
- lengths: int32 [2048], P('dp'), parts along dimension 0, may hold values from 1 to 16
- block_rows: int32 [1024, 2], P('dp'), parts along dimension 0, may hold values from 0 to 511, as said below
- queries: bfloat16 [65536, 2048], P(('dp', 'wide'), 'mp'), parts along dimension 0
- encoder_gain: float32 [896], replicated, may hold values from 0.1 to 1.9
- weight_in: bfloat16 [896, 1792], P('wide', 'mp'), may hold values from -0.1875 to 0.1875
- weight_out: bfloat16 [1792, 896], P('mp', 'wide'), may hold values from -0.125 to 0.125
- weight_key: bfloat16 [896, 2048], P('wide', 'mp'), may hold values from -0.1875 to 0.1875
- weight_value: bfloat16 [896, 2048], P('wide', 'mp'), may hold values from -0.1875 to 0.1875
Outputs:
- attended: bfloat16 [65536, 2048], P(('dp', 'wide'), 'mp'), parts along dimension 0
There are 4 independent parts, one for each index of `dp`. A program takes and returns all parts, laid end to end along the dimension named above; an argument that names none is the same for every part. Nothing has to cross between parts.
Inputs may be any that keep to these rules, and one draw needn't show every extreme that they name: `block_rows`: every neighbour of the part is listed exactly once. The neighbours of one index i of wide (rows i * 8 to (i + 1) * 8 - 1) are listed by the blocks of exactly 8 indices j of wide (blocks j * 4 to (j + 1) * 4 - 1), exactly 1 times by those of each.
All inputs are finite; a program needn't handle non-finite values.
Results may differ from a plain program's by a relative error of at most 0.013.
Values may be sent and summed in bfloat16 or wider, within the bound.
A program may use at most 64 MiB of HBM per device.

v0:
```python
import jax
import jax.numpy as jnp
from jax import lax
from jax.sharding import PartitionSpec as P

HD = 128
BLOCK_LEN = 64
NEIGHBOURS = 2


def attend(query_blocks, key_blocks, value_blocks, usable):
    scores = jnp.einsum(
        "cqhd,ckhd->chqk", query_blocks, key_blocks, preferred_element_type=jnp.float32
    )
    scores = scores * HD ** (-0.5)
    scores = jnp.where(usable[:, None, None, :], scores, -1e30)
    highest = jnp.max(scores, axis=-1, keepdims=True)
    powers = jnp.exp(scores - highest)
    weights = (powers / jnp.sum(powers, axis=-1, keepdims=True)).astype(jnp.bfloat16)
    attended = jnp.einsum(
        "chqk,ckhd->cqhd", weights, value_blocks, preferred_element_type=jnp.float32
    )
    return attended.astype(jnp.bfloat16)


def local(
    neighbour_rows,
    lengths,
    block_rows,
    queries,
    encoder_gain,
    weight_in,
    weight_out,
    weight_key,
    weight_value,
):
    wide_count = lax.axis_size("wide")
    wide_index = lax.axis_index("wide")
    rows_dev, seq_len, width = neighbour_rows.shape
    blocks_dev = queries.shape[0] // BLOCK_LEN
    slot_count = NEIGHBOURS * blocks_dev
    capacity = slot_count // min(slot_count, wide_count // 2)
    token_count = rows_dev * seq_len
    inputs = neighbour_rows.reshape(token_count, width).astype(jnp.float32)
    squares = jnp.mean(inputs * inputs, axis=-1, keepdims=True)
    normed = (inputs * lax.rsqrt(squares + 1e-06) * encoder_gain).astype(jnp.bfloat16)
    columns = normed
    preact = jnp.dot(
        columns,
        lax.all_gather(weight_in, "wide", axis=0, tiled=True),
        preferred_element_type=jnp.float32,
    )
    hidden = jax.nn.gelu(preact).astype(jnp.bfloat16)
    partial_value = jnp.dot(
        hidden,
        lax.all_gather(weight_out, "wide", axis=1, tiled=True),
        preferred_element_type=jnp.float32,
    )
    partial_rows = partial_value.reshape(rows_dev, seq_len, width)
    residual = inputs.reshape(rows_dev, seq_len, width)
    summed = lax.psum(partial_rows, "mp")
    encoded = (residual + summed).astype(jnp.bfloat16)
    piece_len = encoded.shape[1]
    all_slots = block_rows.reshape(-1)
    own_ids = wide_index * rows_dev + jnp.arange(rows_dev, dtype=jnp.int32)
    matches = all_slots[None, :] == own_ids[:, None]
    slot_index = jnp.sum(
        jnp.where(matches, jnp.arange(all_slots.shape[0], dtype=jnp.int32)[None, :], 0), axis=1
    )
    owners = slot_index // slot_count
    row_order = jnp.arange(rows_dev, dtype=jnp.int32)
    earlier = (owners[None, :] == owners[:, None]) & (row_order[None, :] < row_order[:, None])
    targets = owners * capacity + jnp.sum(earlier.astype(jnp.int32), axis=1)
    placing = (
        jnp.arange(wide_count * capacity, dtype=jnp.int32)[:, None] == targets[None, :]
    ).astype(jnp.bfloat16)
    outgoing = jnp.einsum(
        "sr,rtd->std", placing, encoded, preferred_element_type=jnp.float32
    ).astype(jnp.bfloat16)
    outgoing = outgoing.reshape(wide_count, capacity, piece_len, width)
    incoming = lax.all_to_all(outgoing, "wide", split_axis=0, concat_axis=0, tiled=True)
    own_slots = lax.dynamic_slice_in_dim(
        block_rows, wide_index * blocks_dev, blocks_dev, 0
    ).reshape(-1)
    sources = own_slots // rows_dev
    local_rows = own_slots % rows_dev
    before = (sources[None, :] == sources[:, None]) & (local_rows[None, :] < local_rows[:, None])
    positions = sources * capacity + jnp.sum(before.astype(jnp.int32), axis=1)
    arrived = jnp.take(incoming.reshape(wide_count * capacity, piece_len, width), positions, axis=0)
    key_input = arrived.reshape(slot_count * seq_len, width)
    columns = key_input
    key_sum = jnp.dot(
        columns,
        lax.all_gather(weight_key, "wide", axis=0, tiled=True),
        preferred_element_type=jnp.float32,
    )
    value_sum = jnp.dot(
        columns,
        lax.all_gather(weight_value, "wide", axis=0, tiled=True),
        preferred_element_type=jnp.float32,
    )
    heads_dev = weight_key.shape[1] // HD
    key_blocks = key_sum.astype(jnp.bfloat16).reshape(
        blocks_dev, NEIGHBOURS * seq_len, heads_dev, HD
    )
    value_blocks = value_sum.astype(jnp.bfloat16).reshape(
        blocks_dev, NEIGHBOURS * seq_len, heads_dev, HD
    )
    own_lengths = jnp.take(lengths, own_slots).reshape(blocks_dev, NEIGHBOURS)
    usable = jnp.arange(seq_len, dtype=jnp.int32)[None, None, :] < own_lengths[:, :, None]
    usable = usable.reshape(blocks_dev, NEIGHBOURS * seq_len)
    query_blocks = queries.reshape(blocks_dev, BLOCK_LEN, heads_dev, HD)
    attended = attend(query_blocks, key_blocks, value_blocks, usable)
    return attended.reshape(blocks_dev * BLOCK_LEN, heads_dev * HD)


def solution(mesh):
    in_specs = (
        P(("dp", "wide"), None, None),
        P("dp"),
        P("dp", None),
        P(("dp", "wide"), "mp"),
        P(),
        P("wide", "mp"),
        P("mp", "wide"),
        P("wide", "mp"),
        P("wide", "mp"),
    )
    out_specs = P(("dp", "wide"), "mp")
    return jax.shard_map(local, mesh=mesh, in_specs=in_specs, out_specs=out_specs, check_vma=False)
```

profile of v0, /device:TPU:1, one launch (start us, length us, event | category | flops | bytes accessed | tf_op | source)
XLA Modules:
  0.0 648.0 jit_solution(7102105835542322948)
XLA Ops:
  6.5 0.7 all-gather.9.cloned.1.call-update
  7.3 0.7 all-gather.11.cloned.1.call-update
  8.1 1.1 multiply_reduce_fusion
  9.2 1.8 fusion.18
  11.0 136.3 %all-gather.9.cloned.1.call-done = bf16[64,14,896]{2,1,0:T(8,128)(2,1)} async-done(((bf16[1,14,896]{2,1,0:T(8,128)(2,1)}), bf16[64,14,896]{2,1,0:T(8,128)(2,1)}) %all-gather.9.cloned.1.call-update) | async-done | bytes 1605648 | tf_op jit(solution)/shard_map/all_gather | solution.py:50
  147.3 2.5 reshape.349
  149.8 137.1 %all-gather.11.cloned.1.call-done = bf16[64,14,896]{2,1,0:T(8,128)(2,1)} async-done(((bf16[1,14,896]{2,1,0:T(8,128)(2,1)}), bf16[64,14,896]{2,1,0:T(8,128)(2,1)}) %all-gather.11.cloned.1.call-update) | async-done | bytes 1605648 | tf_op jit(solution)/shard_map/all_gather | solution.py:56
  286.9 2.5 reshape.351
  289.5 2.7 fusion.22
  292.2 0.5 all-gather.15.cloned.1.call-update
  293.1 0.2 select_reduce_fusion
  293.3 0.2 convert_reduce_fusion
  293.5 45.0 %all-reduce.2.cloned.1.call-done = f32[8,16,896]{2,1,0:T(8,128)} async-done(((f32[8,16,896]{2,1,0:T(8,128)}), f32[8,16,896]{2,1,0:T(8,128)}) %all-reduce.2.cloned.1.call-update) | async-done | bytes 458768 | tf_op jit(solution)/shard_map/psum | solution.py:61
  338.5 1.1 add_convert_fusion
  339.5 0.8 convert_bitcast_fusion
  340.3 2.3 copy.34
  342.6 14.7 %all-to-all-start = ((bf16[64,1,16,896]{3,2,1,0:T(8,128)(2,1)}), bf16[64,1,16,896]{3,2,1,0:T(8,128)(2,1)}, u32[]{:S(2)}, u32[]{:S(2)}) async-start(bf16[64,1,16,896]{3,2,1,0:T(8,128)(2,1)} %copy.34), calls=%async_computation | async-start | bytes 3670016 | tf_op jit(solution)/shard_map/all_to_all | solution.py:81
  357.3 0.5 all-gather.13.cloned.1.call-update
  358.1 0.2 convert_reduce_fusion.1
  358.5 0.6 gather_fusion.1
  359.6 132.2 %all-gather.15.cloned.1.call-done = bf16[64,14,1024]{2,1,0:T(8,128)(2,1)} async-done(((bf16[1,14,1024]{2,1,0:T(8,128)(2,1)}), bf16[64,14,1024]{2,1,0:T(8,128)(2,1)}) %all-gather.15.cloned.1.call-update) | async-done | bytes 1835024 | tf_op jit(solution)/shard_map/all_gather | solution.py:94
  491.8 3.9 reshape.355
  495.6 136.3 %all-gather.13.cloned.1.call-done = bf16[64,14,1024]{2,1,0:T(8,128)(2,1)} async-done(((bf16[1,14,1024]{2,1,0:T(8,128)(2,1)}), bf16[64,14,1024]{2,1,0:T(8,128)(2,1)}) %all-gather.13.cloned.1.call-update) | async-done | bytes 1835024 | tf_op jit(solution)/shard_map/all_gather | solution.py:99
  631.9 2.6 reshape.353
  634.6 2.1 gather_fusion
  636.8 2.0 fusion.7
  638.8 0.4 fusion.5
  639.2 0.2 fusion.40
  639.3 0.4 fusion.6
  639.9 0.4 fusion.3
  640.2 0.3 copy.38
  640.6 0.9 copy.52
  (43 shorter events, 1.6 us)
Async XLA Ops:
  6.5 351.9 %copy-start = (s32[512]{0:T(512)S(1)}, s32[512]{0:T(512)}, u32[]{:S(2)}) copy-start(s32[512]{0:T(512)} %param.10) | copy-start | bytes 6148
  6.5 140.8 %all-gather.9.cloned.1.call-start = ((), (), s32[]{:S(2)}) async-start(), calls=%async_computation.2 | async-start | bytes 1863680 | tf_op jit(solution)/shard_map/all_gather | solution.py:50
  7.3 279.7 %all-gather.11.cloned.1.call-start = ((), (), s32[]{:S(2)}) async-start(), calls=%async_computation.3 | async-start | bytes 1863680 | tf_op jit(solution)/shard_map/all_gather | solution.py:56
  8.0 330.5 %all-reduce.2.cloned.1.call-start = ((), (), s32[]{:S(2)}) async-start(), calls=%async_computation.1 | async-start | bytes 917504 | tf_op jit(solution)/shard_map/psum | solution.py:61
  289.4 3.3 copy-start.3
  289.5 49.0 %copy-start.1 = (bf16[8,16,896]{2,1,0:T(8,128)(2,1)S(1)}, bf16[8,16,896]{2,1,0:T(8,128)(2,1)}, u32[]{:S(2)}) copy-start(bf16[8,16,896]{2,1,0:T(8,128)(2,1)} %param.9) | copy-start | bytes 688132
  292.2 199.6 %all-gather.15.cloned.1.call-start = ((), (), s32[]{:S(2)}) async-start(), calls=%async_computation.5 | async-start | bytes 2129920 | tf_op jit(solution)/shard_map/all_gather | solution.py:94
  342.6 16.9 %copy-start.2 = (bf16[256,1024]{1,0:T(8,128)(2,1)S(1)}, bf16[256,1024]{1,0:T(8,128)(2,1)}, u32[]{:S(2)}) copy-start(bf16[256,1024]{1,0:T(8,128)(2,1)} %param.12) | copy-start | bytes 1572868
  342.6 292.0 %all-to-all-start = ((bf16[64,1,16,896]{3,2,1,0:T(8,128)(2,1)}), bf16[64,1,16,896]{3,2,1,0:T(8,128)(2,1)}, u32[]{:S(2)}, u32[]{:S(2)}) async-start(bf16[64,1,16,896]{3,2,1,0:T(8,128)(2,1)} %copy.34), calls=%async_computation | async-start | bytes 3670016 | tf_op jit(solution)/shard_map/all_to_all | solution.py:81
  357.3 274.7 %all-gather.13.cloned.1.call-start = ((), (), s32[]{:S(2)}) async-start(), calls=%async_computation.4 | async-start | bytes 2129920 | tf_op jit(solution)/shard_map/all_gather | solution.py:99
Sparse Core Ops, SparseCore 0:
  10.3 136.9 all-gather.8
  150.3 136.6 all-gather.10
  292.3 46.1 all-reduce.1
  341.7 150.0 all-gather.14
  495.0 136.9 all-gather.12
where the time goes:
time: 657 us; the launch traced here: 648 us
  waiting for transfers between devices  589 us (90%)
  local copies, waits for them, and re-layouts  18.9 us (3%)
  starting transfers between devices  14.8 us (2%)
  between operations  13.4 us (2%)
  matrix products  6.61 us (1%)
    all_gather x1, waiting for transfers between devices, local(): lax.all_gather(weight_out, 'wide', axis=1, tiled=True)  137 us
    all_gather x1, waiting for transfers between devices, local(): lax.all_gather(weight_value, 'wide', axis=0, tiled=True)  136 us
    all_gather x1, waiting for transfers between devices, local(): lax.all_gather(weight_in, 'wide', axis=0, tiled=True)  136 us
    all_gather x1, waiting for transfers between devices, local(): lax.all_gather(weight_key, 'wide', axis=0, tiled=True)  132 us
    psum x1, waiting for transfers between devices, local(): summed = lax.psum(partial_rows, 'mp')  45 us
    all_to_all x1, starting transfers between devices, local(): lax.all_to_all(outgoing, 'wide', split_axis=0, concat_axis=0, tiled=True)  14.7 us
  transfers between devices with their start and end apart: 6, of which 5 were waited for; matrix products, arithmetic and copies ran while one was open for 3% of the time, Pallas kernels for 0%

commit v1 on v0

v1 whole, which is shorter than its diff:
```python
import jax
import jax.numpy as jnp
from jax import lax
from jax.experimental import pallas as pl
from jax.experimental.pallas import tpu as pltpu
from jax.sharding import PartitionSpec as P

HD = 128
BLOCK_LEN = 64
NEIGHBOURS = 2
NY, NZ, NX = 4, 16, 4
NW = NZ * NX
MESH = pl.DeviceIdType.MESH
BF16 = jnp.bfloat16
F32 = jnp.float32
WAVES = (0, -4, 4, 8)
SPAN = (0, -1, 1, -2)


def attend(query_blocks, key_blocks, value_blocks, usable):
    scores = jnp.einsum(
        "cqhd,ckhd->chqk", query_blocks, key_blocks, preferred_element_type=jnp.float32
    )
    scores = scores * HD ** (-0.5)
    scores = jnp.where(usable[:, None, None, :], scores, -1e30)
    highest = jnp.max(scores, axis=-1, keepdims=True)
    powers = jnp.exp(scores - highest)
    weights = (powers / jnp.sum(powers, axis=-1, keepdims=True)).astype(jnp.bfloat16)
    attended = jnp.einsum(
        "chqk,ckhd->cqhd", weights, value_blocks, preferred_element_type=jnp.float32
    )
    return attended.astype(jnp.bfloat16)


def kernel(
    rows_ref, index_ref, gain_ref, ff_ref, kv_ref, key_ref, value_ref,
    ff, kv, tiles, held, sorted_rows, arrived, mixed, other,
    ff_z1, ff_z2, ff_x, ff_xf, kv_z1, kv_z2, kv_x, kv_xf, kv_y, kv_yf,
    ff_sent, kv_sent, y_sent, first_sent, first_recv, second_sent, second_recv,
    core_sent, core_recv,
):
    y = lax.axis_index("dp")
    me = lax.axis_index("wide")
    core = lax.axis_index("mp")
    z = me // NX
    x = me % NX
    holder = me % 2 == core

    def slot(zz, xx):
        return ((zz + 2 * NZ) % NZ) * NX + (xx + 2 * NX) % NX

    def plane(yy):
        return (yy + NY) % NY

    barrier = pltpu.get_barrier_semaphore()

    def greet(step, carry):
        pl.semaphore_signal(
            barrier, inc=1, device_id=(y, (me + step) % NW, core), device_id_type=MESH
        )
        return carry

    lax.fori_loop(1, NW, greet, 0)
    for target in ((plane(y + 1), me, core), (plane(y - 1), me, core), (y, me, 1 - core)):
        pl.semaphore_signal(barrier, inc=1, device_id=target, device_id_type=MESH)

    ff[:, pl.ds(me, 1)] = ff_ref[...][:, None]
    kv[pl.ds(y, 1), :, pl.ds(me, 1)] = kv_ref[pl.ds(y, 1)][:, :, None]
    at = lax.broadcasted_iota(jnp.int32, (128, 128), 0)
    of = lax.broadcasted_iota(jnp.int32, (128, 128), 1)
    pairs = (of == (at % 16) // 2 * 16 + at // 16 * 2 + at % 2).astype(F32).astype(BF16)
    in_pairs = jnp.dot(pairs, rows_ref[...], preferred_element_type=F32).astype(BF16)
    feature = lax.broadcasted_iota(jnp.int32, (896, 128), 0)
    lane = lax.broadcasted_iota(jnp.int32, (896, 128), 1)
    for tile in range(8):
        group = tile * 8 + lane // 16
        wanted = jnp.where(lane % 16 < 14, group * 14 + lane % 16, -1)
        pick = (feature == wanted).astype(F32).astype(BF16)
        tiles[tile] = jnp.dot(in_pairs, pick, preferred_element_type=F32).astype(BF16)

    pl.semaphore_wait(barrier, NW + 2)

    def send(src, dst, send_sem, recv_sem, target):
        pltpu.make_async_remote_copy(
            src_ref=src, dst_ref=dst, send_sem=send_sem, recv_sem=recv_sem,
            device_id=target, device_id_type=MESH,
        ).start()

    def wait(ref, sem):
        pltpu.make_async_copy(ref, ref, sem).wait()

    def first(step, carry):
        spot = (me // 2 + step) % (NW // 2)
        target = spot * 2 + core
        src = tiles.at[core * 4 + spot % 4, pl.ds(pl.multiple_of(spot // 4 * 16, 16), 16)]

        @pl.when(target == me)
        def _():
            pltpu.make_async_copy(src, held.at[me], first_recv).start()

        @pl.when(target != me)
        def _():
            send(src, held.at[me], first_sent, first_recv, (y, target, core))

        return carry

    lax.fori_loop(0, NW // 2, first, 0)

    class Ff:
        z1, z2, xs, xf, sent = ff_z1, ff_z2, ff_x, ff_xf, ff_sent

        @staticmethod
        def at(place, count=1):
            return ff.at[:, pl.ds(place, count)]

    class Kv:
        z1, z2, xs, xf, sent = kv_z1, kv_z2, kv_x, kv_xf, kv_sent

        @staticmethod
        def at(place, count=1):
            return kv.at[y, :, pl.ds(place, count)]

    def move(part, place, sem, target):
        send(part.at(place), part.at(place), part.sent, sem, target)

    def z1_send(part):
        for wave, off in ((1, 4), (2, -4), (3, 8)):
            move(part, me, part.z1.at[wave], (y, slot(z + off, x), core))

    def z2_send(part, wave):
        if wave:
            wait(part.at(0), part.z1.at[wave])
        for off in (1, -1, 2):
            move(part, slot(z + WAVES[wave], x), part.z2.at[wave], (y, slot(z + off, x), core))

    def x_send(part, wave):
        wait(part.at(0, 3), part.z2.at[wave])
        for span in SPAN:
            for off in (1, -1):
                move(
                    part, slot(z + WAVES[wave] + span, x), part.xs.at[wave],
                    (y, slot(z, x + off), core),
                )

    def xf_send(part, wave):
        wait(part.at(0, 8), part.xs.at[wave])
        for n, span in enumerate(SPAN):
            off = 1 if n < 2 else -1
            move(
                part, slot(z + WAVES[wave] + span, x - off), part.xf.at[wave],
                (y, slot(z, x + off), core),
            )

    def x_done(part, wave):
        wait(part.at(0, 4), part.xf.at[wave])

    def block(part_y, zz):
        return kv.at[part_y, :, pl.ds(slot(zz, 0), NX)]

    def y_send(wave):
        x_done(Kv, wave)
        for span in SPAN:
            for off in (1, -1):
                ref = block(y, z + WAVES[wave] + span)
                send(ref, ref, y_sent, kv_y.at[wave], (plane(y + off), me, core))

    def yf_send(wave):
        wait(kv.at[0, :, pl.ds(0, 32)], kv_y.at[wave])
        for n, span in enumerate(SPAN):
            off = 1 if n < 2 else -1
            ref = block(plane(y - off), z + WAVES[wave] + span)
            send(ref, ref, y_sent, kv_yf.at[wave], (plane(y + off), me, core))

    def y_done(wave):
        wait(kv.at[0, :, pl.ds(0, 16)], kv_yf.at[wave])

    def permute():
        @pl.when(holder)
        def _():
            wait(held, first_recv)
            rows = held[...].reshape(NW * 16, 128)

            def part(step, carry):
                start = pl.multiple_of(step * 256, 256)
                source = lax.broadcasted_iota(jnp.int32, (256, NW * 16), 1)
                pick = (index_ref[pl.ds(start, 256)] == source).astype(F32).astype(BF16)
                moved = jnp.dot(pick, rows, preferred_element_type=F32).astype(BF16)
                sorted_rows[pl.ds(step * 16, 16)] = moved.reshape(16, 16, 128)
                return carry

            lax.fori_loop(0, 4, part, 0)
            spot = me // 2
            dst = arrived.at[core * 4 + spot % 4, pl.ds(pl.multiple_of(spot // 4 * 16, 16), 16)]

            def second(step, carry):
                target = (me + step) % NW
                send(sorted_rows.at[target], dst, second_sent, second_recv, (y, target, core))
                return carry

            pltpu.make_async_copy(sorted_rows.at[me], dst, second_recv).start()
            lax.fori_loop(1, NW, second, 0)

    def swap_cores():
        wait(arrived.at[pl.ds(0, 4)], second_recv)
        half = arrived.at[pl.ds(core * 4, 4)]
        send(half, half, core_sent.at[0], core_recv.at[0], (y, me, 1 - core))

    z1_send(Kv)
    z1_send(Ff)
    z2_send(Kv, 0)
    z2_send(Ff, 0)
    x_send(Kv, 0)
    x_send(Ff, 0)
    xf_send(Kv, 0)
    z2_send(Kv, 1)
    z2_send(Kv, 2)
    z2_send(Ff, 1)
    y_send(0)
    z2_send(Ff, 2)
    x_send(Kv, 1)
    xf_send(Ff, 0)
    z2_send(Kv, 3)
    z2_send(Ff, 3)
    permute()
    x_send(Kv, 2)
    x_send(Ff, 1)
    xf_send(Kv, 1)
    x_send(Kv, 3)
    x_send(Ff, 2)
    yf_send(0)
    y_send(1)
    xf_send(Kv, 2)
    xf_send(Ff, 1)
    x_send(Ff, 3)
    swap_cores()
    y_send(2)
    xf_send(Kv, 3)
    xf_send(Ff, 2)
    yf_send(1)
    y_send(3)
    xf_send(Ff, 3)
    yf_send(2)

    wait(arrived.at[pl.ds(0, 4)], core_recv.at[0])
    inputs = jnp.concatenate([arrived[tile] for tile in range(8)], axis=1).astype(F32)
    squares = jnp.sum(inputs * inputs, axis=-1, keepdims=True) * (1.0 / 896)
    normed = (inputs * lax.rsqrt(squares + 1e-06) * gain_ref[...]).astype(BF16)
    for wave in range(4):
        x_done(Ff, wave)
    hidden = []
    for start, size in ((0, 256), (256, 256), (512, 256), (768, 128)):
        weight = ff[0, :, :, start : start + size].reshape(NW * 16, size)
        preact = jnp.dot(normed, weight, preferred_element_type=F32)
        hidden.append(jax.nn.gelu(preact).astype(BF16))
    hidden = jnp.concatenate(hidden, axis=1)
    for n in range(4):
        weight = ff[1, n * 16 : (n + 1) * 16].reshape(256, 896)
        mixed[:, n * 256 : (n + 1) * 256] = lax.dot_general(
            hidden, weight, (((1,), (1,)), ((), ())), preferred_element_type=F32
        )
    send(mixed, other, core_sent.at[1], core_recv.at[1], (y, me, 1 - core))
    yf_send(3)
    wait(other, core_recv.at[1])
    encoded = (inputs + (mixed[...] + other[...])).astype(BF16)
    unpair = (of == (at % 16) // 2 * 16 + at // 16 * 2 + at % 2).astype(F32).astype(BF16)
    encoded = jnp.dot(unpair, encoded, preferred_element_type=F32).astype(BF16)
    for wave in range(4):
        y_done(wave)
    for q in range(4):
        for n, out in ((0, key_ref), (1, value_ref)):
            weight = kv[q, n].reshape(NW * 16, 256)
            out[:, q * 256 : (q + 1) * 256] = jnp.dot(
                encoded, weight, preferred_element_type=F32
            ).astype(BF16)

    wait(ff.at[:, pl.ds(0, 63)], ff_sent)
    wait(kv.at[0, :, pl.ds(0, 63)], kv_sent)
    wait(kv.at[pl.ds(0, 3)], y_sent)

    @pl.when(holder)
    def _():
        wait(held.at[pl.ds(0, 31)], first_sent)
        wait(held.at[pl.ds(0, 63)], second_sent)

    @pl.when(jnp.logical_not(holder))
    def _():
        wait(held.at[pl.ds(0, 32)], first_sent)

    wait(arrived.at[pl.ds(0, 4)], core_sent.at[0])
    wait(mixed, core_sent.at[1])


def local(
    neighbour_rows,
    lengths,
    block_rows,
    queries,
    encoder_gain,
    weight_in,
    weight_out,
    weight_key,
    weight_value,
):
    wide_index = lax.axis_index("wide")
    rows_dev, seq_len, width = neighbour_rows.shape
    blocks_dev = queries.shape[0] // BLOCK_LEN
    heads_dev = weight_key.shape[1] // HD
    pad = ((0, 2), (0, 0))
    ff = jnp.stack([jnp.pad(weight_in, pad), jnp.pad(weight_out.T, pad)])
    kv = jnp.stack([jnp.pad(weight_key, pad), jnp.pad(weight_value, pad)])
    kv = kv.reshape(2, 16, 4, 256).transpose(2, 0, 1, 3)
    gain = jnp.pad(encoder_gain.reshape(NW, 14), ((0, 0), (0, 2))).reshape(1, NW * 16)
    index = (block_rows.reshape(-1, 1) * 2 + jnp.arange(2, dtype=jnp.int32)).reshape(-1, 1)
    dma = pltpu.SemaphoreType.DMA
    vmem = pl.BlockSpec(memory_space=pltpu.VMEM)
    keys, values = pl.pallas_call(
        kernel,
        out_shape=[jax.ShapeDtypeStruct((128, 1024), BF16)] * 2,
        in_specs=[vmem] * 5,
        out_specs=[vmem] * 2,
        scratch_shapes=[
            pltpu.VMEM((2, NW, 16, 896), BF16),
            pltpu.VMEM((4, 2, NW, 16, 256), BF16),
            pltpu.VMEM((8, 128, 128), BF16),
            pltpu.VMEM((NW, 16, 128), BF16),
            pltpu.VMEM((NW, 16, 128), BF16),
            pltpu.VMEM((8, 128, 128), BF16),
            pltpu.VMEM((128, 1024), F32),
            pltpu.VMEM((128, 1024), F32),
        ]
        + [dma((4,))] * 10
        + [dma] * 7
        + [dma((2,))] * 2,
        compiler_params=pltpu.CompilerParams(
            collective_id=0, has_side_effects=True, vmem_limit_bytes=48 * 2**20
        ),
        name="route_encode",
    )(neighbour_rows.reshape(rows_dev * seq_len, width), index, gain, ff, kv)
    key_blocks = keys.reshape(blocks_dev, NEIGHBOURS * seq_len, heads_dev, HD)
    value_blocks = values.reshape(blocks_dev, NEIGHBOURS * seq_len, heads_dev, HD)
    own_slots = lax.dynamic_slice_in_dim(
        block_rows, wide_index * blocks_dev, blocks_dev, 0
    ).reshape(-1)
    own_lengths = jnp.take(lengths, own_slots).reshape(blocks_dev, NEIGHBOURS)
    usable = jnp.arange(seq_len, dtype=jnp.int32)[None, None, :] < own_lengths[:, :, None]
    usable = usable.reshape(blocks_dev, NEIGHBOURS * seq_len)
    query_blocks = queries.reshape(blocks_dev, BLOCK_LEN, heads_dev, HD)
    attended = attend(query_blocks, key_blocks, value_blocks, usable)
    return attended.reshape(blocks_dev * BLOCK_LEN, heads_dev * HD)


def solution(mesh):
    in_specs = (
        P(("dp", "wide"), None, None),
        P("dp"),
        P("dp", None),
        P(("dp", "wide"), "mp"),
        P(),
        P("wide", "mp"),
        P("mp", "wide"),
        P("wide", "mp"),
        P("wide", "mp"),
    )
    out_specs = P(("dp", "wide"), "mp")
    return jax.shard_map(local, mesh=mesh, in_specs=in_specs, out_specs=out_specs, check_vma=False)
```

time: 657 us -> 104 us (0.16); the launches traced: 648 us -> 103 us
  waiting for transfers between devices: 589 us -> 0 us
  Pallas kernels: 0 us -> 92.9 us
  starting transfers between devices: 14.8 us -> 0 us
  between operations: 13.4 us -> 0.2 us
  local copies, waits for them, and re-layouts: 18.9 us -> 8.53 us
    all_gather x4 -> x0, waiting for transfers between devices: 542 us -> none  [the longest x1 137 us: local(): lax.all_gather(weight_out, 'wide', axis=1, tiled=True)]
    pallas_call x0 -> x1, Pallas kernels: none -> 92.9 us  [local(): pl.pallas_call(kernel, out_shape=[jax.ShapeDtypeStruct((128, 1024), BF16)...]
    psum x1 -> x0, waiting for transfers between devices: 45 us -> none  [local(): summed = lax.psum(partial_rows, 'mp')]
    all_to_all x1 -> x0, starting transfers between devices: 14.7 us -> none  [local(): lax.all_to_all(outgoing, 'wide', split_axis=0, concat_axis=0, tiled=True)]
  transfers between devices with their start and end apart: 6 -> 0, of which waited for: 5 -> 0; matrix products, arithmetic and copies ran while one was open for 3% -> 0% of each run, Pallas kernels for 0% -> 0%
where the time goes in v1:
time: 104 us; the launch traced here: 103 us
  Pallas kernels  92.9 us (89%)
  local copies, waits for them, and re-layouts  8.53 us (8%)
    pallas_call x1, Pallas kernels, local(): pl.pallas_call(kernel, out_shape=[jax.ShapeDtypeStruct((128, 1024), BF16)...  92.9 us
    unnamed x23, local copies, waits for them, and re-layouts  6.32 us

profile of v1, /device:TPU:1, one launch (start us, length us, event | category | flops | bytes accessed | tf_op | source)
XLA Modules:
  0.0 102.8 jit_solution(13493542975536813266)
XLA Ops:
  0.0 0.7 copy-done.7
  0.7 0.1 constant_dynamic-slice_fusion
  0.8 0.1 copy.23
  0.9 0.1 reshape.127
  1.0 0.1 lt.44
  1.1 0.6 gather_fusion
  1.7 0.1 gather.7
  1.8 0.1 lt.49
  1.9 0.1 lt.50
  2.0 0.6 copy-done.8
  2.6 0.1 reshape.124
  2.7 0.0 copy-start.3
  2.7 0.1 reshape.125.gain_ref
  2.8 0.7 copy-done.3
  3.5 0.0 copy-start.4
  3.5 0.7 copy-done.4
  4.4 0.7 copy-done.5
  5.1 0.0 copy-done.6
  5.1 0.1 copy.14
  5.3 0.1 mul.26
  5.4 0.1 iota_add_fusion
  5.6 0.1 add.60.index_ref
  5.7 0.8 copy-done.1
  6.5 92.9 %route_encode.1 = (bf16[128,1024]{1,0:T(8,128)(2,1)S(1)}, bf16[128,1024]{1,0:T(8,128)(2,1)S(1)}) custom-call(bf16[128,896]{1,0:T(8,128)(2,1)S(1)} %bitcast.32, s32[1024,1]{1,0:T(8,128)S(1)} %add.60.index_ref, f32[1,1024]{1,0:T(1,128)S(1)} %reshape.125.gain_ref, bf16[2,16,896]{2,1,0:T(8,128)(2,1)S(1)} %pad_maximum_fusion.ff_ref, ...), custom_call_target="tpu_custom_call" | custom-call | tf_op jit(solution)/shard_map/route_encode/pallas_call | solution.py:316
  99.4 0.0 copy-start.2
  99.6 0.9 copy-done.2
  100.5 0.1 copy.26
  100.6 0.4 fusion.5
  101.0 0.2 fusion.12
  101.2 0.4 fusion.3
  101.5 0.3 copy.22
  101.9 0.9 copy.35
  (25 shorter events, 0.3 us)
Async XLA Ops:
  0.0 1.1 %copy-start = (s32[512]{0:T(512)S(1)}, s32[512]{0:T(512)}, u32[]{:S(2)}) copy-start(s32[512]{0:T(512)} %param.10) | copy-start | bytes 6148
  0.0 0.7 copy-start.7
  1.9 0.7 copy-start.8
  2.7 0.8 copy-start.3
  3.5 0.8 copy-start.4
  4.3 0.8 copy-start.5
  4.3 0.8 copy-start.6
  5.6 0.9 copy-start.1
  99.4 1.0 %copy-start.2 = (bf16[256,1024]{1,0:T(8,128)(2,1)S(1)}, bf16[256,1024]{1,0:T(8,128)(2,1)}, u32[]{:S(2)}) copy-start(bf16[256,1024]{1,0:T(8,128)(2,1)} %param.12) | copy-start | bytes 1572868

commit v2 on v1

v2 whole, which is shorter than its diff:
```python
import jax
import jax.numpy as jnp
from jax import lax
from jax.experimental import pallas as pl
from jax.experimental.pallas import tpu as pltpu
from jax.sharding import PartitionSpec as P

HD = 128
BLOCK_LEN = 64
NEIGHBOURS = 2
NY, NZ, NX = 4, 16, 4
NW = NZ * NX
MESH = pl.DeviceIdType.MESH
BF16 = jnp.bfloat16
F32 = jnp.float32
WAVES = (0, -4, 4, 8)


def one_hot(mask):
    return mask.astype(F32).astype(BF16)


def kernel(
    rows_hbm, lengths_hbm, blocks_hbm, queries_hbm, gain_hbm,
    in_hbm, out_hbm, key_hbm, value_hbm, attended_ref,
    ff, kv, tiles, held, sorted_rows, arrived, mixed, other, index, gain, keys, values,
    rows_ref, lengths_ref, blocks_ref, queries_ref, gain_ref, in_ref, out_ref, key_ref, value_ref,
    ff_z1, ff_z2, ff_x, ff_xf, kv_z1, kv_z2, kv_x, kv_xf, kv_y, kv_yf,
    ff_sent, kv_sent, y_sent, first_sent, first_recv, second_sent, second_recv,
    core_sent, core_recv, loaded,
):
    y = lax.axis_index("dp")
    me = lax.axis_index("wide")
    core = lax.axis_index("mp")
    z = me // NX
    x = me % NX
    holder = me % 2 == core
    side = 2 - 4 * core
    spans = (0, -1, 1, -side)

    def slot(zz, xx):
        return ((zz + 2 * NZ) % NZ) * NX + (xx + 2 * NX) % NX

    def plane(yy):
        return (yy + NY) % NY

    loads = [
        pltpu.make_async_copy(src, dst, loaded.at[n])
        for n, (src, dst) in enumerate(
            (
                (in_hbm, in_ref), (out_hbm, out_ref), (key_hbm, key_ref), (value_hbm, value_ref),
                (rows_hbm, rows_ref), (gain_hbm, gain_ref), (blocks_hbm, blocks_ref),
                (lengths_hbm, lengths_ref), (queries_hbm, queries_ref),
            )
        )
    ]
    for load in loads:
        load.start()
    barrier = pltpu.get_barrier_semaphore()

    def greet(step, carry):
        pl.semaphore_signal(
            barrier, inc=1, device_id=(y, (me + step) % NW, core), device_id_type=MESH
        )
        return carry

    lax.fori_loop(1, NW, greet, 0)
    for target in ((plane(y + 1), me, core), (plane(y - 1), me, core), (y, me, 1 - core)):
        pl.semaphore_signal(barrier, inc=1, device_id=target, device_id_type=MESH)

    for load in loads[:4]:
        load.wait()
    row = lax.broadcasted_iota(jnp.int32, (16, 14), 0)
    pad = one_hot(row == lax.broadcasted_iota(jnp.int32, (16, 14), 1))

    def padded(shard):
        return jnp.dot(pad, shard, preferred_element_type=F32).astype(BF16)

    ff[0, pl.ds(me, 1)] = padded(in_ref[...])[None]
    ff[1, pl.ds(me, 1)] = padded(out_ref[...])[None]
    for n, ref in ((0, key_ref), (1, value_ref)):
        shard = padded(ref[:, pl.ds(pl.multiple_of(y * 256, 256), 256)])
        kv[pl.ds(y, 1), n, pl.ds(me, 1)] = shard[None, None]

    pl.semaphore_wait(barrier, NW + 2)

    def prepare():
        for load in loads[4:8]:
            load.wait()
        at = lax.broadcasted_iota(jnp.int32, (128, 128), 0)
        of = lax.broadcasted_iota(jnp.int32, (128, 128), 1)
        pairs = one_hot(of == (at % 16) // 2 * 16 + at // 16 * 2 + at % 2)
        in_pairs = jnp.dot(pairs, rows_ref[...], preferred_element_type=F32).astype(BF16)
        feature = lax.broadcasted_iota(jnp.int32, (896, 128), 0)
        lane = lax.broadcasted_iota(jnp.int32, (1, 128), 1)
        whole = gain_ref[...]
        high = whole.astype(BF16).astype(F32)
        middle = (whole - high).astype(BF16).astype(F32)
        low = whole - high - middle
        term = lax.broadcasted_iota(jnp.int32, (16, 896), 0)
        terms = jnp.where(
            term == 0, high, jnp.where(term == 1, middle, jnp.where(term == 2, low, 0.0))
        ).astype(BF16)
        for tile in range(8):
            wanted = jnp.where(
                lane % 16 < 14, (tile * 8 + lane // 16) * 14 + lane % 16, -1
            )
            pick = one_hot(feature == wanted)
            tiles[tile] = jnp.dot(in_pairs, pick, preferred_element_type=F32).astype(BF16)
            gain[:, tile * 128 : (tile + 1) * 128] = jnp.sum(
                jnp.dot(terms, pick, preferred_element_type=F32), axis=0, keepdims=True
            )

    def number():
        listed = blocks_ref[...]
        block = lax.broadcasted_iota(jnp.int32, (NW * 16, 256), 1)
        place = lax.broadcasted_iota(jnp.int32, (NW * 16, 256), 0)
        spread = one_hot(block == place // 4)
        halves = []
        for value in (listed // 2, listed % 2):
            value = jnp.broadcast_to(value[:, None], (NEIGHBOURS, 8, 256)).reshape(16, 256)
            halves.append(
                lax.dot_general(
                    spread, value.astype(F32).astype(BF16), (((1,), (1,)), ((), ())),
                    preferred_element_type=F32,
                )
            )
        both = 4.0 * halves[0] + 2.0 * halves[1]
        place = lax.broadcasted_iota(jnp.int32, (NW * 16, 1), 0)
        half = (place % 2).astype(F32)
        index[...] = jnp.where(place // 2 % 2 == 0, both[:, 0:1], both[:, 8:9]) + half

    def send(src, dst, send_sem, recv_sem, target):
        pltpu.make_async_remote_copy(
            src_ref=src, dst_ref=dst, send_sem=send_sem, recv_sem=recv_sem,
            device_id=target, device_id_type=MESH,
        ).start()

    def wait(ref, sem):
        pltpu.make_async_copy(ref, ref, sem).wait()

    def first(step, carry):
        spot = (me // 2 + step) % (NW // 2)
        target = spot * 2 + core
        src = tiles.at[core * 4 + spot % 4, pl.ds(pl.multiple_of(spot // 4 * 16, 16), 16)]

        @pl.when(target == me)
        def _():
            pltpu.make_async_copy(src, held.at[me], first_recv).start()

        @pl.when(target != me)
        def _():
            send(src, held.at[me], first_sent, first_recv, (y, target, core))

        return carry

    def route():
        lax.fori_loop(0, NW // 2, first, 0)


    class Ff:
        z1, z2, xs, xf, sent = ff_z1, ff_z2, ff_x, ff_xf, ff_sent

        @staticmethod
        def at(place, count=1):
            return ff.at[:, pl.ds(place, count)]

    class Kv:
        z1, z2, xs, xf, sent = kv_z1, kv_z2, kv_x, kv_xf, kv_sent

        @staticmethod
        def at(place, count=1):
            return kv.at[y, :, pl.ds(place, count)]

    def move(part, place, sem, target):
        send(part.at(place), part.at(place), part.sent, sem, target)

    def z1_send(part):
        for wave, off in ((1, 4), (2, -4), (3, 8)):
            move(part, me, part.z1.at[wave], (y, slot(z + off, x), core))

    def z2_send(part, wave):
        if wave:
            wait(part.at(0), part.z1.at[wave])
        for off in (1, -1, side):
            move(part, slot(z + WAVES[wave], x), part.z2.at[wave], (y, slot(z + off, x), core))

    def x_send(part, wave):
        wait(part.at(0, 3), part.z2.at[wave])
        for span in spans:
            for off in (1, -1):
                move(
                    part, slot(z + WAVES[wave] + span, x), part.xs.at[wave],
                    (y, slot(z, x + off), core),
                )

    def xf_send(part, wave):
        wait(part.at(0, 8), part.xs.at[wave])
        for n, span in enumerate(spans):
            off = 1 if n < 2 else -1
            move(
                part, slot(z + WAVES[wave] + span, x - off), part.xf.at[wave],
                (y, slot(z, x + off), core),
            )

    def x_done(part, wave):
        wait(part.at(0, 4), part.xf.at[wave])

    def block(part_y, zz):
        return kv.at[part_y, :, pl.ds(slot(zz, 0), NX)]

    def y_send(wave):
        x_done(Kv, wave)
        for span in spans:
            for off in (1, -1):
                ref = block(y, z + WAVES[wave] + span)
                send(ref, ref, y_sent, kv_y.at[wave], (plane(y + off), me, core))

    def yf_send(wave):
        wait(kv.at[0, :, pl.ds(0, 32)], kv_y.at[wave])
        for n, span in enumerate(spans):
            off = 1 if n < 2 else -1
            ref = block(plane(y - off), z + WAVES[wave] + span)
            send(ref, ref, y_sent, kv_yf.at[wave], (plane(y + off), me, core))

    def y_done(wave):
        wait(kv.at[0, :, pl.ds(0, 16)], kv_yf.at[wave])

    def permute():
        number()

        @pl.when(holder)
        def _():
            wait(held, first_recv)
            rows = held[...].reshape(NW * 16, 128)

            def part(step, carry):
                start = pl.multiple_of(step * 256, 256)
                source = lax.broadcasted_iota(jnp.int32, (256, NW * 16), 1).astype(F32)
                pick = one_hot(index[pl.ds(start, 256)] == source)
                moved = jnp.dot(pick, rows, preferred_element_type=F32).astype(BF16)
                sorted_rows[pl.ds(step * 16, 16)] = moved.reshape(16, 16, 128)
                return carry

            lax.fori_loop(0, 4, part, 0)
            spot = me // 2
            dst = arrived.at[core * 4 + spot % 4, pl.ds(pl.multiple_of(spot // 4 * 16, 16), 16)]

            def second(step, carry):
                target = (me + step) % NW
                send(sorted_rows.at[target], dst, second_sent, second_recv, (y, target, core))
                return carry

            pltpu.make_async_copy(sorted_rows.at[me], dst, second_recv).start()
            lax.fori_loop(1, NW, second, 0)

    def swap_cores():
        wait(arrived.at[pl.ds(0, 4)], second_recv)
        half = arrived.at[pl.ds(core * 4, 4)]
        send(half, half, core_sent.at[0], core_recv.at[0], (y, me, 1 - core))

    z2_send(Kv, 0)
    z2_send(Ff, 0)
    prepare()
    route()
    z1_send(Kv)
    z1_send(Ff)
    x_send(Kv, 0)
    x_send(Ff, 0)
    xf_send(Kv, 0)
    z2_send(Kv, 1)
    z2_send(Kv, 2)
    y_send(0)
    z2_send(Kv, 3)
    x_send(Kv, 1)
    z2_send(Ff, 1)
    xf_send(Ff, 0)
    z2_send(Ff, 2)
    x_send(Kv, 2)
    xf_send(Kv, 1)
    z2_send(Ff, 3)
    x_send(Ff, 1)
    yf_send(0)
    y_send(1)
    permute()
    x_send(Kv, 3)
    xf_send(Kv, 2)
    xf_send(Ff, 1)
    x_send(Ff, 2)
    y_send(2)
    yf_send(1)
    xf_send(Kv, 3)
    x_send(Ff, 3)
    xf_send(Ff, 2)
    swap_cores()
    y_send(3)
    xf_send(Ff, 3)
    yf_send(2)

    wait(arrived.at[pl.ds(0, 4)], core_recv.at[0])
    inputs = jnp.concatenate([arrived[tile] for tile in range(8)], axis=1).astype(F32)
    squares = jnp.sum(inputs * inputs, axis=-1, keepdims=True) * (1.0 / 896)
    normed = (inputs * lax.rsqrt(squares + 1e-06) * gain[...]).astype(BF16)
    for wave in range(4):
        x_done(Ff, wave)
    hidden = []
    for start, size in ((0, 256), (256, 256), (512, 256), (768, 128)):
        weight = ff[0, :, :, start : start + size].reshape(NW * 16, size)
        preact = jnp.dot(normed, weight, preferred_element_type=F32)
        hidden.append(jax.nn.gelu(preact).astype(BF16))
    hidden = jnp.concatenate(hidden, axis=1)
    for n in range(4):
        weight = ff[1, n * 16 : (n + 1) * 16].reshape(256, 896)
        mixed[:, n * 256 : (n + 1) * 256] = lax.dot_general(
            hidden, weight, (((1,), (1,)), ((), ())), preferred_element_type=F32
        )
    send(mixed, other, core_sent.at[1], core_recv.at[1], (y, me, 1 - core))
    yf_send(3)
    wait(other, core_recv.at[1])
    encoded = (inputs + (mixed[...] + other[...])).astype(BF16)
    for wave in range(4):
        y_done(wave)
    for q in range(4):
        for n, out in ((0, keys), (1, values)):
            weight = kv[q, n].reshape(NW * 16, 256)
            out[:, q * 256 : (q + 1) * 256] = jnp.dot(
                encoded, weight, preferred_element_type=F32
            ).astype(BF16)

    loads[8].wait()
    mine = index[pl.ds(pl.multiple_of(me * 16, 16), 16)]
    source = lax.broadcasted_iota(jnp.int32, (16, 512), 1).astype(F32) * 2.0
    hit = (mine == source) | (mine == source + 1.0)
    live = jnp.where(hit, lengths_ref[...].astype(F32), 0.0)
    live = jnp.sum(live, axis=1, keepdims=True)
    lane = lax.broadcasted_iota(jnp.int32, (16, 128), 1)
    spot = lax.broadcasted_iota(jnp.int32, (16, 128), 0)
    live = jnp.sum(jnp.where(lane % 16 == spot, live, 0.0), axis=0, keepdims=True)
    lane = lax.broadcasted_iota(jnp.int32, (256, 128), 1)
    block_at = lax.broadcasted_iota(jnp.int32, (256, 128), 0) // BLOCK_LEN
    token = (lane // 16 * 2 + lane % 2).astype(F32)
    usable = (block_at == lane % 16 // 4) & (token < live)
    for head in range(8):
        part = slice(head * HD, (head + 1) * HD)
        scores = lax.dot_general(
            queries_ref[:, part], keys[:, part], (((1,), (1,)), ((), ())),
            preferred_element_type=F32,
        )
        scores = jnp.where(usable, scores * HD ** (-0.5), -1e30)
        powers = jnp.exp(scores - jnp.max(scores, axis=-1, keepdims=True))
        weights = (powers / jnp.sum(powers, axis=-1, keepdims=True)).astype(BF16)
        attended_ref[:, part] = jnp.dot(
            weights, values[:, part], preferred_element_type=F32
        ).astype(BF16)

    wait(ff.at[:, pl.ds(0, 63)], ff_sent)
    wait(kv.at[0, :, pl.ds(0, 63)], kv_sent)
    wait(kv.at[pl.ds(0, 3)], y_sent)

    @pl.when(holder)
    def _():
        wait(held.at[pl.ds(0, 31)], first_sent)
        wait(held.at[pl.ds(0, 63)], second_sent)

    @pl.when(jnp.logical_not(holder))
    def _():
        wait(held.at[pl.ds(0, 32)], first_sent)

    wait(arrived.at[pl.ds(0, 4)], core_sent.at[0])
    wait(mixed, core_sent.at[1])


def local(
    neighbour_rows,
    lengths,
    block_rows,
    queries,
    encoder_gain,
    weight_in,
    weight_out,
    weight_key,
    weight_value,
):
    dma = pltpu.SemaphoreType.DMA
    vmem = pl.BlockSpec(memory_space=pltpu.VMEM)
    return pl.pallas_call(
        kernel,
        out_shape=jax.ShapeDtypeStruct(queries.shape, BF16),
        in_specs=[pl.BlockSpec(memory_space=pl.ANY)] * 9,
        out_specs=vmem,
        scratch_shapes=[
            pltpu.VMEM((2, NW, 16, 896), BF16),
            pltpu.VMEM((4, 2, NW, 16, 256), BF16),
            pltpu.VMEM((8, 128, 128), BF16),
            pltpu.VMEM((NW, 16, 128), BF16),
            pltpu.VMEM((NW, 16, 128), BF16),
            pltpu.VMEM((8, 128, 128), BF16),
            pltpu.VMEM((128, 1024), F32),
            pltpu.VMEM((128, 1024), F32),
            pltpu.VMEM((NW * 16, 1), F32),
            pltpu.VMEM((1, NW * 16), F32),
            pltpu.VMEM((128, 1024), BF16),
            pltpu.VMEM((128, 1024), BF16),
            pltpu.VMEM((128, 896), BF16),
            pltpu.VMEM((1, 512), jnp.int32),
            pltpu.VMEM((2, 256), jnp.int32),
            pltpu.VMEM((256, 1024), BF16),
            pltpu.VMEM((1, 896), F32),
            pltpu.VMEM((14, 896), BF16),
            pltpu.VMEM((14, 896), BF16),
            pltpu.VMEM((14, 1024), BF16),
            pltpu.VMEM((14, 1024), BF16),
        ]
        + [dma((4,))] * 10
        + [dma] * 7
        + [dma((2,))] * 2
        + [dma((9,))],
        compiler_params=pltpu.CompilerParams(
            collective_id=0, has_side_effects=True, vmem_limit_bytes=60 * 2**20
        ),
        name="route_encode_attend",
    )(
        neighbour_rows.reshape(-1, neighbour_rows.shape[-1]),
        lengths.reshape(1, -1),
        block_rows.T,
        queries,
        encoder_gain.reshape(1, -1),
        weight_in,
        weight_out.T,
        weight_key,
        weight_value,
    )


def solution(mesh):
    in_specs = (
        P(("dp", "wide"), None, None),
        P("dp"),
        P("dp", None),
        P(("dp", "wide"), "mp"),
        P(),
        P("wide", "mp"),
        P("mp", "wide"),
        P("wide", "mp"),
        P("wide", "mp"),
    )
    out_specs = P(("dp", "wide"), "mp")
    return jax.shard_map(local, mesh=mesh, in_specs=in_specs, out_specs=out_specs, check_vma=False)
```

time: 104 us -> 89.1 us (0.86)
  Pallas kernels: 92.9 us -> 84.6 us
  local copies, waits for them, and re-layouts: 8.53 us -> 3.14 us
    pallas_call x1, Pallas kernels: 92.9 us -> 84.6 us  [local(): pl.pallas_call(kernel, out_shape=jax.ShapeDtypeStruct(queries.shape, BF16...]
    unnamed x23 -> x3, local copies, waits for them, and re-layouts: 6.32 us -> 2.56 us
where the time goes in v2:
time: 89.1 us; the launch traced here: 87.8 us
  Pallas kernels  84.6 us (95%)
  local copies, waits for them, and re-layouts  3.14 us (4%)
    pallas_call x1, Pallas kernels, local(): pl.pallas_call(kernel, out_shape=jax.ShapeDtypeStruct(queries.shape, BF16...  84.6 us
    unnamed x3, local copies, waits for them, and re-layouts  2.56 us

profile of v2, /device:TPU:1, one launch (start us, length us, event | category | flops | bytes accessed | tf_op | source)
XLA Modules:
  0.0 87.8 jit_solution(7910196469962975758)
XLA Ops:
  0.0 0.0 copy-start
  0.0 0.7 copy-done
  0.7 0.6 reshape.11.gain_hbm
  1.3 84.6 %route_encode_attend.1 = bf16[256,1024]{1,0:T(8,128)(2,1)} custom-call(bf16[128,896]{1,0:T(8,128)(2,1)} %bitcast.4, s32[1,512]{1,0:T(1,128)} %bitcast.6, s32[2,256]{1,0:T(2,128)} %bitcast.7, bf16[256,1024]{1,0:T(8,128)(2,1)} %queries_hbm.1, f32[1,896]{1,0:T(1,128)} %reshape.11.gain_hbm, bf16[14,896]{1,0:T(8,128)(2,1)} %in_hbm.1, bf16[14,896]{1,0:T(8,128)(2,1)} %bitcast.5, ...), custom_call_target="tpu_custom_call" | custom-call | tf_op jit(solution)/shard_map/route_encode_attend/pallas_call | solution.py:386
  85.9 1.9 %copy.11 = bf16[256,1024]{1,0:T(8,128)(2,1)} copy(bf16[256,1024]{1,0:T(8,128)(2,1)} %route_encode_attend.1) | data formatting | bytes 1048576
Async XLA Ops:
  0.0 0.7 copy-start

commit v3 on v2

--- a/solution.py
+++ b/solution.py
@@ -93,7 +93,7 @@
         in_pairs = jnp.dot(pairs, rows_ref[...], preferred_element_type=F32).astype(BF16)
         feature = lax.broadcasted_iota(jnp.int32, (896, 128), 0)
         lane = lax.broadcasted_iota(jnp.int32, (1, 128), 1)
-        whole = gain_ref[...]
+        whole = gain_ref[...].reshape(1, 896)
         high = whole.astype(BF16).astype(F32)
         middle = (whole - high).astype(BF16).astype(F32)
         low = whole - high - middle
@@ -259,43 +259,44 @@
         half = arrived.at[pl.ds(core * 4, 4)]
         send(half, half, core_sent.at[0], core_recv.at[0], (y, me, 1 - core))
 
+    z1_send(Kv)
     z2_send(Kv, 0)
     z2_send(Ff, 0)
-    prepare()
-    route()
-    z1_send(Kv)
-    z1_send(Ff)
-    x_send(Kv, 0)
-    x_send(Ff, 0)
-    xf_send(Kv, 0)
     z2_send(Kv, 1)
     z2_send(Kv, 2)
-    y_send(0)
+    x_send(Kv, 0)
+    z1_send(Ff)
+    x_send(Ff, 0)
     z2_send(Kv, 3)
+    x_send(Kv, 2)
+    prepare()
     x_send(Kv, 1)
+    xf_send(Kv, 0)
     z2_send(Ff, 1)
     xf_send(Ff, 0)
+    route()
+    xf_send(Kv, 2)
+    xf_send(Kv, 1)
+    x_send(Kv, 3)
+    y_send(0)
+    x_send(Ff, 1)
     z2_send(Ff, 2)
-    x_send(Kv, 2)
-    xf_send(Kv, 1)
+    y_send(1)
+    y_send(2)
     z2_send(Ff, 3)
-    x_send(Ff, 1)
     yf_send(0)
-    y_send(1)
+    xf_send(Kv, 3)
+    x_send(Ff, 2)
+    xf_send(Ff, 1)
     permute()
-    x_send(Kv, 3)
-    xf_send(Kv, 2)
-    xf_send(Ff, 1)
-    x_send(Ff, 2)
-    y_send(2)
+    x_send(Ff, 3)
+    y_send(3)
     yf_send(1)
-    xf_send(Kv, 3)
-    x_send(Ff, 3)
+    yf_send(2)
     xf_send(Ff, 2)
+    xf_send(Ff, 3)
     swap_cores()
-    y_send(3)
-    xf_send(Ff, 3)
-    yf_send(2)
+    yf_send(3)
 
     wait(arrived.at[pl.ds(0, 4)], core_recv.at[0])
     inputs = jnp.concatenate([arrived[tile] for tile in range(8)], axis=1).astype(F32)
@@ -311,13 +312,16 @@
     hidden = jnp.concatenate(hidden, axis=1)
     for n in range(4):
         weight = ff[1, n * 16 : (n + 1) * 16].reshape(256, 896)
-        mixed[:, n * 256 : (n + 1) * 256] = lax.dot_general(
+        mixed[n] = lax.dot_general(
             hidden, weight, (((1,), (1,)), ((), ())), preferred_element_type=F32
         )
-    send(mixed, other, core_sent.at[1], core_recv.at[1], (y, me, 1 - core))
-    yf_send(3)
-    wait(other, core_recv.at[1])
-    encoded = (inputs + (mixed[...] + other[...])).astype(BF16)
+        send(mixed.at[n], other.at[n], core_sent.at[n + 1], core_recv.at[n + 1], (y, me, 1 - core))
+    encoded = []
+    for n in range(4):
+        wait(other.at[n], core_recv.at[n + 1])
+        part = inputs[:, n * 256 : (n + 1) * 256] + (mixed[n] + other[n])
+        encoded.append(part.astype(BF16))
+    encoded = jnp.concatenate(encoded, axis=1)
     for wave in range(4):
         y_done(wave)
     for q in range(4):
@@ -367,7 +371,8 @@
         wait(held.at[pl.ds(0, 32)], first_sent)
 
     wait(arrived.at[pl.ds(0, 4)], core_sent.at[0])
-    wait(mixed, core_sent.at[1])
+    for n in range(4):
+        wait(mixed.at[n], core_sent.at[n + 1])
 
 
 def local(
@@ -395,8 +400,8 @@
             pltpu.VMEM((NW, 16, 128), BF16),
             pltpu.VMEM((NW, 16, 128), BF16),
             pltpu.VMEM((8, 128, 128), BF16),
-            pltpu.VMEM((128, 1024), F32),
-            pltpu.VMEM((128, 1024), F32),
+            pltpu.VMEM((4, 128, 256), F32),
+            pltpu.VMEM((4, 128, 256), F32),
             pltpu.VMEM((NW * 16, 1), F32),
             pltpu.VMEM((1, NW * 16), F32),
             pltpu.VMEM((128, 1024), BF16),
@@ -405,7 +410,7 @@
             pltpu.VMEM((1, 512), jnp.int32),
             pltpu.VMEM((2, 256), jnp.int32),
             pltpu.VMEM((256, 1024), BF16),
-            pltpu.VMEM((1, 896), F32),
+            pltpu.VMEM((896,), F32),
             pltpu.VMEM((14, 896), BF16),
             pltpu.VMEM((14, 896), BF16),
             pltpu.VMEM((14, 1024), BF16),
@@ -413,7 +418,7 @@
         ]
         + [dma((4,))] * 10
         + [dma] * 7
-        + [dma((2,))] * 2
+        + [dma((5,))] * 2
         + [dma((9,))],
         compiler_params=pltpu.CompilerParams(
             collective_id=0, has_side_effects=True, vmem_limit_bytes=60 * 2**20
@@ -424,7 +429,7 @@
         lengths.reshape(1, -1),
         block_rows.T,
         queries,
-        encoder_gain.reshape(1, -1),
+        encoder_gain,
         weight_in,
         weight_out.T,
         weight_key,

time: 89.1 us -> 78.5 us (0.88); the launches traced: 87.8 us -> 78.3 us
  Pallas kernels: 84.6 us -> 76.4 us
  local copies, waits for them, and re-layouts: 3.14 us -> 1.87 us
    pallas_call x1, Pallas kernels: 84.6 us -> 76.4 us  [local(): pl.pallas_call(kernel, out_shape=jax.ShapeDtypeStruct(queries.shape, BF16...]
    unnamed x3 -> x1, local copies, waits for them, and re-layouts: 2.56 us -> 1.87 us
where the time goes in v3:
time: 78.5 us; the launch traced here: 78.3 us
  Pallas kernels  76.4 us (97%)
  local copies, waits for them, and re-layouts  1.87 us (2%)
    pallas_call x1, Pallas kernels, local(): pl.pallas_call(kernel, out_shape=jax.ShapeDtypeStruct(queries.shape, BF16...  76.4 us
    unnamed x1, local copies, waits for them, and re-layouts  1.87 us

profile of v3, /device:TPU:1, one launch (start us, length us, event | category | flops | bytes accessed | tf_op | source)
XLA Modules:
  0.0 78.3 jit_solution(16509921592123215957)
XLA Ops:
  0.0 76.4 %route_encode_attend.1 = bf16[256,1024]{1,0:T(8,128)(2,1)} custom-call(bf16[128,896]{1,0:T(8,128)(2,1)} %bitcast.4, s32[1,512]{1,0:T(1,128)} %bitcast.6, s32[2,256]{1,0:T(2,128)} %bitcast.7, bf16[256,1024]{1,0:T(8,128)(2,1)} %queries_hbm.1, f32[896]{0:T(1024)} %gain_hbm.1, bf16[14,896]{1,0:T(8,128)(2,1)} %in_hbm.1, bf16[14,896]{1,0:T(8,128)(2,1)} %bitcast.5, ...), custom_call_target="tpu_custom_call" | custom-call | tf_op jit(solution)/shard_map/route_encode_attend/pallas_call | solution.py:391
  76.4 1.9 %copy.11 = bf16[256,1024]{1,0:T(8,128)(2,1)} copy(bf16[256,1024]{1,0:T(8,128)(2,1)} %route_encode_attend.1) | data formatting | bytes 1048576

commit v4 on v3

--- a/solution.py
+++ b/solution.py
@@ -27,7 +27,7 @@
     rows_ref, lengths_ref, blocks_ref, queries_ref, gain_ref, in_ref, out_ref, key_ref, value_ref,
     ff_z1, ff_z2, ff_x, ff_xf, kv_z1, kv_z2, kv_x, kv_xf, kv_y, kv_yf,
     ff_sent, kv_sent, y_sent, first_sent, first_recv, second_sent, second_recv,
-    core_sent, core_recv, loaded,
+    core_sent, core_recv, loaded, far_sent, far_recv,
 ):
     y = lax.axis_index("dp")
     me = lax.axis_index("wide")
@@ -65,7 +65,10 @@
         return carry
 
     lax.fori_loop(1, NW, greet, 0)
-    for target in ((plane(y + 1), me, core), (plane(y - 1), me, core), (y, me, 1 - core)):
+    for target in (
+        (plane(y + 1), me, core), (plane(y - 1), me, core), (plane(y + 2), me, core),
+        (y, me, 1 - core),
+    ):
         pl.semaphore_signal(barrier, inc=1, device_id=target, device_id_type=MESH)
 
     for load in loads[:4]:
@@ -82,7 +85,7 @@
         shard = padded(ref[:, pl.ds(pl.multiple_of(y * 256, 256), 256)])
         kv[pl.ds(y, 1), n, pl.ds(me, 1)] = shard[None, None]
 
-    pl.semaphore_wait(barrier, NW + 2)
+    pl.semaphore_wait(barrier, NW + 3)
 
     def prepare():
         for load in loads[4:8]:
@@ -93,10 +96,10 @@
         in_pairs = jnp.dot(pairs, rows_ref[...], preferred_element_type=F32).astype(BF16)
         feature = lax.broadcasted_iota(jnp.int32, (896, 128), 0)
         lane = lax.broadcasted_iota(jnp.int32, (1, 128), 1)
-        whole = gain_ref[...].reshape(1, 896)
-        high = whole.astype(BF16).astype(F32)
-        middle = (whole - high).astype(BF16).astype(F32)
-        low = whole - high - middle
+        exact = gain_ref[...].reshape(1, 896)
+        high = exact.astype(BF16).astype(F32)
+        middle = (exact - high).astype(BF16).astype(F32)
+        low = exact - high - middle
         term = lax.broadcasted_iota(jnp.int32, (16, 896), 0)
         terms = jnp.where(
             term == 0, high, jnp.where(term == 1, middle, jnp.where(term == 2, low, 0.0))
@@ -175,19 +178,68 @@
     def move(part, place, sem, target):
         send(part.at(place), part.at(place), part.sent, sem, target)
 
-    def z1_send(part):
-        for wave, off in ((1, 4), (2, -4), (3, 8)):
-            move(part, me, part.z1.at[wave], (y, slot(z + off, x), core))
+    def z1_send(wave):
+        off = (4, -4, 8)[wave - 1]
+        move(Kv, me, kv_z1.at[wave], (y, slot(z + off, x), core))
+
+    turn = (y + core) % 2
+    whole = y < 2
+    fetched = ff_z1.at[1 + turn]
+
+    def fetch():
+        @pl.when(whole)
+        def _():
+            ref = ff.at[:, pl.ds(me, 1)]
+            send(ref, ref, far_sent, fetched, (y, slot(z + 4 - 8 * turn, x), core))
+
+        @pl.when(jnp.logical_not(whole))
+        def _():
+            ref = ff.at[y % 2, pl.ds(me, 1)]
+            send(ref, ref, far_sent, far_recv, (y, slot(z + 8, x), core))
+
+    def spread():
+        @pl.when(whole)
+        def _():
+            wait(ff.at[:, pl.ds(0, 1)], fetched)
+            ref = ff.at[:, pl.ds(slot(z - 4 + 8 * turn, x), 1)]
+            for off in (1, -1, 2):
+                send(ref, ref, far_sent, fetched, (plane(y + off), me, core))
+
+        @pl.when(jnp.logical_not(whole))
+        def _():
+            wait(ff.at[0, pl.ds(0, 1)], far_recv)
+            ref = ff.at[y % 2, pl.ds(slot(z + 8, x), 1)]
+            for off in (1, -1, 2):
+                send(ref, ref, far_sent, ff_z1.at[3], (plane(y + off), me, core))
 
     def z2_send(part, wave):
-        if wave:
+        if part is Kv and wave:
             wait(part.at(0), part.z1.at[wave])
+        elif wave == 3:
+
+            @pl.when(whole)
+            def _():
+                wait(ff.at[:, pl.ds(0, 1)], ff_z1.at[3])
+
+            @pl.when(jnp.logical_not(whole))
+            def _():
+                wait(ff.at[0, pl.ds(0, 1)], ff_z1.at[3])
+        elif wave:
+
+            @pl.when(jnp.logical_not(whole & (turn == wave - 1)))
+            def _():
+                wait(ff.at[:, pl.ds(0, 1)], ff_z1.at[wave])
+
         for off in (1, -1, side):
             move(part, slot(z + WAVES[wave], x), part.z2.at[wave], (y, slot(z + off, x), core))
 
+    def own_send(part, wave):
+        for off in (1, -1):
+            move(part, slot(z + WAVES[wave], x), part.xs.at[wave], (y, slot(z, x + off), core))
+
     def x_send(part, wave):
         wait(part.at(0, 3), part.z2.at[wave])
-        for span in spans:
+        for span in spans[1:]:
             for off in (1, -1):
                 move(
                     part, slot(z + WAVES[wave] + span, x), part.xs.at[wave],
@@ -259,44 +311,55 @@
         half = arrived.at[pl.ds(core * 4, 4)]
         send(half, half, core_sent.at[0], core_recv.at[0], (y, me, 1 - core))
 
-    z1_send(Kv)
     z2_send(Kv, 0)
+    z1_send(1)
+    z1_send(2)
     z2_send(Ff, 0)
+    own_send(Ff, 0)
+    own_send(Kv, 0)
+    fetch()
+    x_send(Kv, 0)
+    prepare()
+    z1_send(3)
+    z2_send(Kv, 2)
+    own_send(Kv, 2)
+    x_send(Ff, 0)
     z2_send(Kv, 1)
-    z2_send(Kv, 2)
-    x_send(Kv, 0)
-    z1_send(Ff)
-    x_send(Ff, 0)
+    xf_send(Kv, 0)
+    route()
+    own_send(Kv, 1)
+    x_send(Kv, 2)
+    spread()
+    xf_send(Ff, 0)
     z2_send(Kv, 3)
-    x_send(Kv, 2)
-    prepare()
+    y_send(0)
     x_send(Kv, 1)
-    xf_send(Kv, 0)
+    own_send(Kv, 3)
+    xf_send(Kv, 2)
     z2_send(Ff, 1)
-    xf_send(Ff, 0)
-    route()
-    xf_send(Kv, 2)
+    x_send(Kv, 3)
+    z2_send(Ff, 3)
+    own_send(Ff, 3)
     xf_send(Kv, 1)
-    x_send(Kv, 3)
-    y_send(0)
+    own_send(Ff, 1)
+    z2_send(Ff, 2)
+    y_send(2)
+    xf_send(Kv, 3)
+    own_send(Ff, 2)
     x_send(Ff, 1)
-    z2_send(Ff, 2)
     y_send(1)
-    y_send(2)
-    z2_send(Ff, 3)
+    x_send(Ff, 3)
+    permute()
+    x_send(Ff, 2)
+    y_send(3)
+    yf_send(2)
+    xf_send(Ff, 3)
     yf_send(0)
-    xf_send(Kv, 3)
-    x_send(Ff, 2)
     xf_send(Ff, 1)
-    permute()
-    x_send(Ff, 3)
-    y_send(3)
+    yf_send(3)
+    xf_send(Ff, 2)
     yf_send(1)
-    yf_send(2)
-    xf_send(Ff, 2)
-    xf_send(Ff, 3)
     swap_cores()
-    yf_send(3)
 
     wait(arrived.at[pl.ds(0, 4)], core_recv.at[0])
     inputs = jnp.concatenate([arrived[tile] for tile in range(8)], axis=1).astype(F32)
@@ -357,7 +420,16 @@
             weights, values[:, part], preferred_element_type=F32
         ).astype(BF16)
 
-    wait(ff.at[:, pl.ds(0, 63)], ff_sent)
+    wait(ff.at[:, pl.ds(0, 60)], ff_sent)
+
+    @pl.when(whole)
+    def _():
+        wait(ff.at[:, pl.ds(0, 4)], far_sent)
+
+    @pl.when(jnp.logical_not(whole))
+    def _():
+        wait(ff.at[:, pl.ds(0, 2)], far_sent)
+
     wait(kv.at[0, :, pl.ds(0, 63)], kv_sent)
     wait(kv.at[pl.ds(0, 3)], y_sent)
 
@@ -419,7 +491,7 @@
         + [dma((4,))] * 10
         + [dma] * 7
         + [dma((5,))] * 2
-        + [dma((9,))],
+        + [dma((9,)), dma, dma],
         compiler_params=pltpu.CompilerParams(
             collective_id=0, has_side_effects=True, vmem_limit_bytes=60 * 2**20
         ),

time: 78.5 us -> 75.3 us (0.959)
  the two profiles are of different devices: /device:TPU:1 before, /device:TPU:65 now
where the time goes in v4:
time: 75.3 us; the launch traced here: 75.1 us
  Pallas kernels  73.3 us (97%)
  local copies, waits for them, and re-layouts  1.87 us (2%)
    pallas_call x1, Pallas kernels, local(): pl.pallas_call(kernel, out_shape=jax.ShapeDtypeStruct(queries.shape, BF16...  73.3 us
    unnamed x1, local copies, waits for them, and re-layouts  1.87 us

profile of v4, /device:TPU:65, one launch (start us, length us, event | category | flops | bytes accessed | tf_op | source)
XLA Modules:
  0.0 75.1 jit_solution(1960774985953884002)
XLA Ops:
  0.0 73.3 %route_encode_attend.1 = bf16[256,1024]{1,0:T(8,128)(2,1)} custom-call(bf16[128,896]{1,0:T(8,128)(2,1)} %bitcast.4, s32[1,512]{1,0:T(1,128)} %bitcast.6, s32[2,256]{1,0:T(2,128)} %bitcast.7, bf16[256,1024]{1,0:T(8,128)(2,1)} %queries_hbm.1, f32[896]{0:T(1024)} %gain_hbm.1, bf16[14,896]{1,0:T(8,128)(2,1)} %in_hbm.1, bf16[14,896]{1,0:T(8,128)(2,1)} %bitcast.5, ...), custom_call_target="tpu_custom_call" | custom-call | tf_op jit(solution)/shard_map/route_encode_attend/pallas_call | solution.py:463
  73.3 1.9 %copy.11 = bf16[256,1024]{1,0:T(8,128)(2,1)} copy(bf16[256,1024]{1,0:T(8,128)(2,1)} %route_encode_attend.1) | data formatting | bytes 1048576

commit v5 on v4

--- a/solution.py
+++ b/solution.py
@@ -24,6 +24,7 @@
     rows_hbm, lengths_hbm, blocks_hbm, queries_hbm, gain_hbm,
     in_hbm, out_hbm, key_hbm, value_hbm, attended_ref,
     ff, kv, tiles, held, sorted_rows, arrived, mixed, other, index, gain, keys, values,
+    picks,
     rows_ref, lengths_ref, blocks_ref, queries_ref, gain_ref, in_ref, out_ref, key_ref, value_ref,
     ff_z1, ff_z2, ff_x, ff_xf, kv_z1, kv_z2, kv_x, kv_xf, kv_y, kv_yf,
     ff_sent, kv_sent, y_sent, first_sent, first_recv, second_sent, second_recv,
@@ -59,12 +60,16 @@
     barrier = pltpu.get_barrier_semaphore()
 
     def greet(step, carry):
-        pl.semaphore_signal(
-            barrier, inc=1, device_id=(y, (me + step) % NW, core), device_id_type=MESH
-        )
+        for far in (NW // 2 + step, NW // 2 - step):
+            pl.semaphore_signal(
+                barrier, inc=1, device_id=(y, (me + far) % NW, core), device_id_type=MESH
+            )
         return carry
 
-    lax.fori_loop(1, NW, greet, 0)
+    pl.semaphore_signal(
+        barrier, inc=1, device_id=(y, (me + NW // 2) % NW, core), device_id_type=MESH
+    )
+    lax.fori_loop(1, NW // 2, greet, 0)
     for target in (
         (plane(y + 1), me, core), (plane(y - 1), me, core), (plane(y + 2), me, core),
         (y, me, 1 - core),
@@ -143,7 +148,8 @@
         pltpu.make_async_copy(ref, ref, sem).wait()
 
     def first(step, carry):
-        spot = (me // 2 + step) % (NW // 2)
+        apart = NW // 4 + (step + 1) // 2 * (1 - 2 * (step % 2))
+        spot = (me // 2 + apart) % (NW // 2)
         target = spot * 2 + core
         src = tiles.at[core * 4 + spot % 4, pl.ds(pl.multiple_of(spot // 4 * 16, 16), 16)]
 
@@ -278,9 +284,21 @@
     def y_done(wave):
         wait(kv.at[0, :, pl.ds(0, 16)], kv_yf.at[wave])
 
+    def mark():
+        number()
+
+        @pl.when(holder)
+        def _():
+            source = lax.broadcasted_iota(jnp.int32, (256, NW * 16), 1).astype(F32)
+
+            def part(step, carry):
+                start = pl.multiple_of(step * 256, 256)
+                picks[pl.ds(start, 256)] = one_hot(index[pl.ds(start, 256)] == source)
+                return carry
+
+            lax.fori_loop(0, 4, part, 0)
+
     def permute():
-        number()
-
         @pl.when(holder)
         def _():
             wait(held, first_recv)
@@ -288,8 +306,7 @@
 
             def part(step, carry):
                 start = pl.multiple_of(step * 256, 256)
-                source = lax.broadcasted_iota(jnp.int32, (256, NW * 16), 1).astype(F32)
-                pick = one_hot(index[pl.ds(start, 256)] == source)
+                pick = picks[pl.ds(start, 256)]
                 moved = jnp.dot(pick, rows, preferred_element_type=F32).astype(BF16)
                 sorted_rows[pl.ds(step * 16, 16)] = moved.reshape(16, 16, 128)
                 return carry
@@ -299,7 +316,8 @@
             dst = arrived.at[core * 4 + spot % 4, pl.ds(pl.multiple_of(spot // 4 * 16, 16), 16)]
 
             def second(step, carry):
-                target = (me + step) % NW
+                apart = NW // 2 + step // 2 * (1 - 2 * (step % 2))
+                target = (me + apart) % NW
                 send(sorted_rows.at[target], dst, second_sent, second_recv, (y, target, core))
                 return carry
 
@@ -329,6 +347,7 @@
     route()
     own_send(Kv, 1)
     x_send(Kv, 2)
+    mark()
     spread()
     xf_send(Ff, 0)
     z2_send(Kv, 3)
@@ -478,6 +497,7 @@
             pltpu.VMEM((1, NW * 16), F32),
             pltpu.VMEM((128, 1024), BF16),
             pltpu.VMEM((128, 1024), BF16),
+            pltpu.VMEM((NW * 16, NW * 16), BF16),
             pltpu.VMEM((128, 896), BF16),
             pltpu.VMEM((1, 512), jnp.int32),
             pltpu.VMEM((2, 256), jnp.int32),

time: 75.3 us -> 73.8 us (0.980)
  the two profiles are of different devices: /device:TPU:65 before, /device:TPU:1 now
where the time goes in v5:
time: 73.8 us; the launch traced here: 73.7 us
  Pallas kernels  71.8 us (97%)
  local copies, waits for them, and re-layouts  1.87 us (3%)
    pallas_call x1, Pallas kernels, local(): pl.pallas_call(kernel, out_shape=jax.ShapeDtypeStruct(queries.shape, BF16...  71.8 us
    unnamed x1, local copies, waits for them, and re-layouts  1.87 us

profile of v5, /device:TPU:1, one launch (start us, length us, event | category | flops | bytes accessed | tf_op | source)
XLA Modules:
  0.0 73.7 jit_solution(11684333244329486746)
XLA Ops:
  0.0 71.8 %route_encode_attend.1 = bf16[256,1024]{1,0:T(8,128)(2,1)} custom-call(bf16[128,896]{1,0:T(8,128)(2,1)} %bitcast.4, s32[1,512]{1,0:T(1,128)} %bitcast.6, s32[2,256]{1,0:T(2,128)} %bitcast.7, bf16[256,1024]{1,0:T(8,128)(2,1)} %queries_hbm.1, f32[896]{0:T(1024)} %gain_hbm.1, bf16[14,896]{1,0:T(8,128)(2,1)} %in_hbm.1, bf16[14,896]{1,0:T(8,128)(2,1)} %bitcast.5, ...), custom_call_target="tpu_custom_call" | custom-call | tf_op jit(solution)/shard_map/route_encode_attend/pallas_call | solution.py:482
  71.8 1.9 %copy.11 = bf16[256,1024]{1,0:T(8,128)(2,1)} copy(bf16[256,1024]{1,0:T(8,128)(2,1)} %route_encode_attend.1) | data formatting | bytes 1048576

commit v6 on v5

--- a/solution.py
+++ b/solution.py
@@ -380,6 +380,19 @@
     yf_send(1)
     swap_cores()
 
+    mine = index[pl.ds(pl.multiple_of(me * 16, 16), 16)]
+    source = lax.broadcasted_iota(jnp.int32, (16, 512), 1).astype(F32) * 2.0
+    hit = (mine == source) | (mine == source + 1.0)
+    live = jnp.where(hit, lengths_ref[...].astype(F32), 0.0)
+    live = jnp.sum(live, axis=1, keepdims=True)
+    lane = lax.broadcasted_iota(jnp.int32, (16, 128), 1)
+    spot = lax.broadcasted_iota(jnp.int32, (16, 128), 0)
+    live = jnp.sum(jnp.where(lane % 16 == spot, live, 0.0), axis=0, keepdims=True)
+    lane = lax.broadcasted_iota(jnp.int32, (256, 128), 1)
+    block_at = lax.broadcasted_iota(jnp.int32, (256, 128), 0) // BLOCK_LEN
+    token = (lane // 16 * 2 + lane % 2).astype(F32)
+    usable = (block_at == lane % 16 // 4) & (token < live)
+
     wait(arrived.at[pl.ds(0, 4)], core_recv.at[0])
     inputs = jnp.concatenate([arrived[tile] for tile in range(8)], axis=1).astype(F32)
     squares = jnp.sum(inputs * inputs, axis=-1, keepdims=True) * (1.0 / 896)
@@ -414,18 +427,6 @@
             ).astype(BF16)
 
     loads[8].wait()
-    mine = index[pl.ds(pl.multiple_of(me * 16, 16), 16)]
-    source = lax.broadcasted_iota(jnp.int32, (16, 512), 1).astype(F32) * 2.0
-    hit = (mine == source) | (mine == source + 1.0)
-    live = jnp.where(hit, lengths_ref[...].astype(F32), 0.0)
-    live = jnp.sum(live, axis=1, keepdims=True)
-    lane = lax.broadcasted_iota(jnp.int32, (16, 128), 1)
-    spot = lax.broadcasted_iota(jnp.int32, (16, 128), 0)
-    live = jnp.sum(jnp.where(lane % 16 == spot, live, 0.0), axis=0, keepdims=True)
-    lane = lax.broadcasted_iota(jnp.int32, (256, 128), 1)
-    block_at = lax.broadcasted_iota(jnp.int32, (256, 128), 0) // BLOCK_LEN
-    token = (lane // 16 * 2 + lane % 2).astype(F32)
-    usable = (block_at == lane % 16 // 4) & (token < live)
     for head in range(8):
         part = slice(head * HD, (head + 1) * HD)
         scores = lax.dot_general(

time: 73.8 us -> 73.8 us (level)
  no operation moved by 1% of the time
where the time goes in v6:
time: 73.8 us; the launch traced here: 73.6 us
  Pallas kernels  71.8 us (97%)
  local copies, waits for them, and re-layouts  1.87 us (3%)
    pallas_call x1, Pallas kernels, local(): pl.pallas_call(kernel, out_shape=jax.ShapeDtypeStruct(queries.shape, BF16...  71.8 us
    unnamed x1, local copies, waits for them, and re-layouts  1.87 us

profile of v6, /device:TPU:1, one launch (start us, length us, event | category | flops | bytes accessed | tf_op | source)
XLA Modules:
  0.0 73.6 jit_solution(8500822766226920402)
XLA Ops:
  0.0 71.8 %route_encode_attend.1 = bf16[256,1024]{1,0:T(8,128)(2,1)} custom-call(bf16[128,896]{1,0:T(8,128)(2,1)} %bitcast.4, s32[1,512]{1,0:T(1,128)} %bitcast.6, s32[2,256]{1,0:T(2,128)} %bitcast.7, bf16[256,1024]{1,0:T(8,128)(2,1)} %queries_hbm.1, f32[896]{0:T(1024)} %gain_hbm.1, bf16[14,896]{1,0:T(8,128)(2,1)} %in_hbm.1, bf16[14,896]{1,0:T(8,128)(2,1)} %bitcast.5, ...), custom_call_target="tpu_custom_call" | custom-call | tf_op jit(solution)/shard_map/route_encode_attend/pallas_call | solution.py:483
  71.8 1.9 %copy.11 = bf16[256,1024]{1,0:T(8,128)(2,1)} copy(bf16[256,1024]{1,0:T(8,128)(2,1)} %route_encode_attend.1) | data formatting | bytes 1048576
